TPU v7x, 128 devices: a whole 4x4x4 slice. The times are simulated.
128 devices in a mesh: tok: 32 (over y, x, core), col: 4 (over z).
Axes of the slice: x: 4, y: 4, z: 4, core: 2. Of those that a mesh axis runs over, the one named last changes fastest.
Arguments:
- samples: bfloat16 [131072, 1024], P('tok', 'col')
- lengths: int32 [32, 16], replicated, may hold values from 1 to 4065, as said below
- sketch: bfloat16 [1024, 1024], replicated
Outputs:
- latent_basis: float32 [1024, 1024], P('tok', 'col')
Inputs may be any that keep to these rules, and one draw needn't show every extreme that they name: Each buffer's lengths sum to at most 4096; the sums of buffer i and of the buffer half the tok axis away from it add up to exactly 4096.
All inputs are finite; a program needn't handle non-finite values.
Results may differ from a plain program's by a relative error of at most 0.00037.
Values may be sent and summed in bfloat16 or wider, within the bound.
A program may use at most 128 MiB of HBM per device.

v0:
```python
import functools
import math

import jax
import jax.numpy as jnp
from jax import lax
from jax.experimental import pallas as pl
from jax.experimental.pallas import tpu as pltpu
from jax.sharding import PartitionSpec as P

F32, BF16 = jnp.float32, jnp.bfloat16
MESH = pl.DeviceIdType.MESH
G_STREAMS = ((0, 256), (256, 256), (512, 128))
C_STREAMS = ((0, 256), (256, 384), (640, 384))
G_PLACES = ((0, 512), (1, 384), (1, 0), (0, 0))
SUBS = 4

class Place:
    def __init__(self):
        self.tok = lax.axis_index("tok")
        self.core = lax.rem(self.tok, 2)
        self.at = (lax.axis_index("col"), self.tok // 8, lax.rem(self.tok // 2, 4))

    def device(self, at, core):
        z, y, x = at
        return ((y * 4 + x) * 2 + core, z)

    def mate(self):
        return self.device(self.at, 1 - self.core)

    def peer(self, axis, d):
        at = list(self.at)
        at[axis] = lax.rem(at[axis] + d, 4)
        return self.device(at, self.core)

    def step(self, axis, d):
        return lax.rem(self.at[axis] + d + 4, 4)

def remote(src, dst, ssem, rsem, dev):
    return pltpu.make_async_remote_copy(src_ref=src, dst_ref=dst, send_sem=ssem, recv_sem=rsem, device_id=dev, device_id_type=MESH)

def pick(axis, p, lanes):
    idx = [slice(None)] * 3
    idx[axis] = p
    return tuple(idx) + (slice(None), pl.ds(*lanes))

def greet(place):
    barrier = pltpu.get_barrier_semaphore()
    pl.semaphore_signal(barrier, inc=1, device_id=place.mate(), device_id_type=MESH)
    for axis in range(3):
        for d in range(1, 4):
            pl.semaphore_signal(barrier, inc=1, device_id=place.peer(axis, d), device_id_type=MESH)
    pl.semaphore_wait(barrier, 10)

class Reduction:
    def __init__(self, place, streams, acc, r1, a1, r2, a2, r3, a3, ps, pr):
        self.place, self.streams = place, streams
        self.acc, self.r, self.a = acc, (r1, r2, r3), (a1, a2, a3)
        self.ps, self.pr = ps, pr
        self.copies = {}

    def order(self, s):
        return (s, (s + 1) % 3, (s + 2) % 3)

    def sub(self, s, phase, p):
        if phase == 0:
            return pick(s, p, self.streams[s])
        if phase == 1 and s == 1:
            return (slice(None), p)
        return (p,)

    def source(self, s, phase):
        return self.acc if phase == 0 else self.a[phase - 1][s]

    def send(self, phase, s):
        axis = self.order(s)[phase]
        for d in (2, 1, 3):
            src = self.source(s, phase).at[self.sub(s, phase, self.place.step(axis, d))]
            c = remote(src, self.r[phase][s].at[d - 1], self.ps.at[phase, s, d - 1], self.pr.at[phase, s, d - 1], self.place.peer(axis, d))
            c.start()
            self.copies[phase, s, d] = c

    def gather(self, phase, s):
        axis = self.order(s)[phase]
        total = self.source(s, phase)[self.sub(s, phase, self.place.step(axis, 0))]
        for d in range(1, 4):
            self.copies[phase, s, d].wait_recv()
        r = self.r[phase][s]
        self.a[phase][s][...] = (total + r[0]) + (r[1] + r[2])

    def share(self, s):
        axis = self.order(s)[2]
        for d in (2, 1, 3):
            c = remote(self.a[1][s], self.r[2][s].at[d - 1], self.ps.at[2, s, d - 1], self.pr.at[2, s, d - 1], self.place.peer(axis, d))
            c.start()
            self.copies[2, s, d] = c

    def shared(self, s):
        for d in range(1, 4):
            self.copies[2, s, d].wait_recv()
        r = self.r[2][s]
        return (self.a[1][s][...] + r[0]) + (r[1] + r[2])

    def finish(self):
        for c in self.copies.values():
            c.wait_send()

class Spread:
    def __init__(self, red, full, out, ss, rs, fs, fr, ws):
        self.red, self.full, self.place = red, full, red.place
        self.ss, self.rs, self.fs, self.fr, self.ws = ss, rs, fs, fr, ws
        self.out = out
        self.sends, self.writes = [], []

    def region(self, s, fixed, core):
        idx = [slice(None)] * 3
        for axis, p in fixed.items():
            idx[axis] = p
        return self.full.at[(core,) + tuple(idx) + (slice(None), pl.ds(*self.red.streams[s]))]

    def seed(self, s):
        idx = [slice(None)] * 3
        for axis in self.red.order(s)[:2]:
            idx[axis] = self.place.at[axis]
        o, n = self.red.streams[s]
        self.full[(self.place.core,) + tuple(idx) + (slice(None), slice(o, o + n))] = self.red.shared(s)

    def fixed(self, s, phase, d):
        axes = self.red.order(s)[:3 - phase]
        f = {a: self.place.at[a] for a in axes}
        f[axes[-1]] = self.place.step(axes[-1], -d)
        return f, axes[-1]

    def copy(self, phase, s, d, held):
        f, axis = self.fixed(s, phase, held)
        reg = self.region(s, f, self.place.core)
        return remote(reg, reg, self.ss.at[phase, s, d - 1], self.rs.at[phase, s, d - 1], self.place.peer(axis, d))

    def send(self, phase, s):
        for d in (2, 1, 3):
            c = self.copy(phase, s, d, 0)
            c.start()
            self.sends.append(c)

    def arrived(self, phase, s, d):
        self.copy(phase, s, d, d).wait_recv()

    def wait(self, phase, s):
        for d in range(1, 4):
            self.arrived(phase, s, d)

    def passing(self, s, d, core):
        f, _ = self.fixed(s, 2, d)
        reg = self.region(s, f, core)
        return remote(reg, reg, self.fs.at[s, d], self.fr.at[s, d], self.place.mate())

    def write(self, s, d, core):
        f, _ = self.fixed(s, 2, d)
        idx = [slice(None)] * 3
        for axis, p in f.items():
            idx[axis] = p
        idx = (core,) + tuple(idx) + (slice(None), pl.ds(*self.red.streams[s]))
        c = pltpu.make_async_copy(self.full.at[idx], self.out.at[idx], self.ws.at[s, d, 0 if core is self.place.core else 1])
        c.start()
        self.writes.append(c)

    def forward(self, s, d):
        c = self.passing(s, d, self.place.core)
        c.start()
        self.sends.append(c)
        self.write(s, d, self.place.core)

    def finish(self):
        for d in (0, 1, 3, 2):
            for s in range(3):
                self.passing(s, d, 1 - self.place.core).wait_recv()
                self.write(s, d, 1 - self.place.core)
        for c in self.sends:
            c.wait_send()
        for c in self.writes:
            c.wait()

class Rows:
    def __init__(self, place, x, held, loc, zs, zr, ms, mr):
        self.place, self.x, self.held = place, x, held
        self.loc, self.zs, self.zr, self.ms, self.mr = loc, zs, zr, ms, mr
        self.step = held.shape[2] // SUBS

    def rows(self, sub):
        return pl.ds(sub * self.step, self.step)

    def slot(self, core, d, sub):
        return self.held.at[core, self.place.step(0, -d), self.rows(sub)]

    def own(self, sub):
        return pltpu.make_async_copy(self.x.at[self.place.at[0], self.rows(sub)], self.slot(self.place.core, 0, sub), self.loc.at[sub])

    def across(self, d, sub):
        return remote(self.x.at[self.place.step(0, d), self.rows(sub)], self.slot(self.place.core, 0, sub),
                      self.zs.at[sub, d - 1], self.zr.at[sub, d - 1], self.place.peer(0, d))

    def passing(self, d, sub, core):
        src = self.x.at[self.place.at[0], self.rows(sub)] if d == 0 else self.slot(core, d, sub)
        return remote(src, self.slot(core, d, sub), self.ms.at[sub, d], self.mr.at[sub, d], self.place.mate())

    def take(self, sub):
        self.own(sub).wait()
        for d in (1, 3, 2):
            remote(self.slot(self.place.core, d, sub), self.slot(self.place.core, d, sub),
                   self.zs.at[sub, d - 1], self.zr.at[sub, d - 1], self.place.peer(0, d)).wait_recv()
            self.passing(d, sub, self.place.core).start()

    def take_other(self, sub):
        for d in range(4):
            self.passing(d, sub, 1 - self.place.core).wait_recv()

    def finish(self):
        for sub in range(SUBS):
            for d in range(4):
                self.passing(d, sub, self.place.core).wait_send()
                if d:
                    self.across(d, sub).wait_send()

def over_rows(a, b):
    return lax.dot_general(a, b, (((0,), (0,)), ((), ())), preferred_element_type=F32)

def weights_into(place, lengths, wcol):
    rows = wcol.shape[1]
    assert rows == 1024
    pos = place.at[0] * rows + lax.broadcasted_iota(jnp.int32, (8, 128), 0) * 128 + lax.broadcasted_iota(jnp.int32, (8, 128), 1)
    for k in range(2):
        buf = place.tok - place.core + k
        start = jnp.zeros((8, 128), jnp.int32)
        w = jnp.zeros((8, 128), F32)
        for s in range(lengths.shape[1]):
            count = jnp.full((8, 128), lengths[buf, s], jnp.int32)
            per = lax.rsqrt(1.0 + 4.0 * count.astype(F32) / float(2 * rows))
            w = w + jnp.where((pos >= start) & (pos < start + count), per, 0.0)
            start = start + count
        wt = w.T
        for a in range(8):
            wcol[k, 128 * a:128 * (a + 1)] = jnp.broadcast_to(wt[:, a:a + 1], (128, 128))

def front_kernel(len_ref, x_ref, sk_ref, go_ref, co_ref, held, omega, wcol, sh, sl, gs, cs, full, ss, rs, fs, fr, ws, loc, zs, zr, ms, mr, osem):
    place = Place()
    core = place.core
    rows = Rows(place, x_ref, held, loc, zs, zr, ms, mr)
    g = Reduction(place, G_STREAMS, *gs)
    c = Reduction(place, C_STREAMS, *cs)
    sketch = pltpu.make_async_copy(sk_ref, omega, osem.at[0])
    sketch.start()
    for sub in range(SUBS):
        rows.own(sub).start()
    greet(place)
    for sub in range(SUBS):
        for d in (2, 1, 3):
            rows.across(d, sub).start()
        rows.passing(0, sub, core).start()
    weights_into(place, len_ref, wcol)
    g.acc[...] = jnp.zeros_like(g.acc)
    c.acc[...] = jnp.zeros_like(c.acc)
    sketch.wait()
    step = rows.step

    def project(sub, k, which):
        x = jnp.concatenate([held[which, z, pl.ds(sub * step, step)] for z in range(4)], 1)
        prod = jnp.dot(x, omega[...], preferred_element_type=F32)
        w = wcol[which, pl.ds(sub * step, step)]
        s = prod * jnp.concatenate([w] * (omega.shape[1] // 128), 1)
        hi = s.astype(BF16)
        at = pl.ds((2 * sub + k) * step, step)
        sh[at] = hi
        sl[at] = (s - hi.astype(F32)).astype(BF16)

    def chunk(sub, _):
        rows.take(sub)
        project(sub, 0, core)
        rows.take_other(sub)
        project(sub, 1, 1 - core)
        at = pl.ds(2 * sub * step, 2 * step)
        for i in range(4):
            width = 128 * (i + 1)
            far = pl.ds(pl.multiple_of(core * width, 128), width)
            lh, ll, rh, rl = sh[at, 256 * i:256 * (i + 1)], sl[at, 256 * i:256 * (i + 1)], sh[at, far], sl[at, far]
            v = over_rows(lh, rh) + over_rows(lh, rl) + over_rows(ll, rh)
            half, lane = G_PLACES[i]
            g.acc[2 * half:2 * half + 2, :, :, :, lane:lane + width] += v.reshape(2, 4, 4, 8, width)
        return 0

    lax.fori_loop(0, SUBS, chunk, 0)
    for s in range(3):
        g.send(0, s)

    def cross(sub, _):
        mine = pl.ds(pl.multiple_of(core * 128, 128), 128)
        for k in range(2):
            which = core if k == 0 else 1 - core
            x = jnp.concatenate([held[which, z, pl.ds(sub * step, step), mine] for z in range(4)], 1)
            at = pl.ds((2 * sub + k) * step, step)
            v = over_rows(x, sh[at]) + over_rows(x, sl[at])
            c.acc[...] += v.reshape(4, 4, 4, 8, omega.shape[1])
        return 0

    lax.fori_loop(0, SUBS, cross, 0)
    sp = Spread(g, full, go_ref, ss, rs, fs, fr, ws)
    for s in range(3):
        g.gather(0, s)
        g.send(1, s)
    for s in range(3):
        c.send(0, s)
    for s in range(3):
        g.gather(1, s)
        g.share(s)
    for s in range(3):
        sp.seed(s)
        sp.send(1, s)
    for s in range(3):
        c.gather(0, s)
        c.send(1, s)
    for s in range(3):
        sp.wait(1, s)
        sp.send(2, s)
        sp.forward(s, 0)
    for s in range(3):
        c.gather(1, s)
        c.send(2, s)
    for d in (1, 3, 2):
        for s in range(3):
            sp.arrived(2, s, d)
            sp.forward(s, d)
    for s in range(3):
        c.gather(2, s)
        o, n = C_STREAMS[s]
        co_ref[0:8, o:o + n] = c.a[2][s][...]
    co_ref[8:16, :] = jnp.zeros((8, omega.shape[1]), F32)
    sp.finish()
    rows.finish()
    g.finish()
    c.finish()

def reduce_scratch(streams, last):
    lanes = sum(n for _, n in streams)
    def per(shape):
        return [pltpu.VMEM(shape + (8, n), F32) for _, n in streams]
    dma = pltpu.SemaphoreType.DMA
    return [pltpu.VMEM((4, 4, 4, 8, lanes), F32), per((3, 4, 4)), per((4, 4)), per((3, 4)), per((4,)), per((3,) + last), per(last),
            dma((3, 3, 3)), dma((3, 3, 3))]

def front(lengths, samples, sketch):
    dma = pltpu.SemaphoreType.DMA
    rows, feats = samples.shape
    width = sketch.shape[1]
    chunk = rows // 4
    return pl.pallas_call(
        front_kernel,
        out_shape=(jax.ShapeDtypeStruct((2, 4, 4, 4, 8, 640), F32), jax.ShapeDtypeStruct((16, width), F32)),
        in_specs=[pl.BlockSpec(memory_space=pltpu.SMEM), pl.BlockSpec(memory_space=pl.ANY), pl.BlockSpec(memory_space=pl.ANY)],
        out_specs=(pl.BlockSpec(memory_space=pl.ANY), pl.BlockSpec(memory_space=pltpu.VMEM)),
        scratch_shapes=[pltpu.VMEM((2, 4, chunk, feats), BF16), pltpu.VMEM(sketch.shape, BF16), pltpu.VMEM((2, chunk, 128), F32),
                        pltpu.VMEM((2 * chunk, width), BF16), pltpu.VMEM((2 * chunk, width), BF16),
                        reduce_scratch(G_STREAMS, (4,)), reduce_scratch(C_STREAMS, ()), pltpu.VMEM((2, 4, 4, 4, 8, 640), F32),
                        dma((3, 3, 3)), dma((3, 3, 3)), dma((3, 4)), dma((3, 4)), dma((3, 4, 2)),
                        dma((SUBS,)), dma((SUBS, 3)), dma((SUBS, 3)), dma((SUBS, 4)), dma((SUBS, 4)), dma((1,))],
        compiler_params=pltpu.CompilerParams(collective_id=1, has_side_effects=True, vmem_limit_bytes=56 << 20),
        cost_estimate=pl.CostEstimate(flops=13_000_000_000, bytes_accessed=8 << 20, transcendentals=0),
    )(lengths, samples.reshape(4, chunk, feats), sketch)

def swap_kernel(scale, y_ref, o_ref, got, flat, ssem, rsem):
    place = Place()
    tok = place.tok
    barrier = pltpu.get_barrier_semaphore()
    count = 32
    def hello(d, _):
        pl.semaphore_signal(barrier, inc=1, device_id=(lax.rem(tok + d, count), place.at[0]), device_id_type=MESH)
        return 0
    lax.fori_loop(1, count, hello, 0)
    pl.semaphore_wait(barrier, count - 1)
    def copy(d, owner):
        to = lax.rem(tok + d, count)
        lanes = pl.ds(pl.multiple_of((to // 4) * 128, 128), 128)
        return remote(y_ref.at[0:8, lanes], got.at[lax.rem(owner, 2), owner // 2], ssem.at[d], rsem.at[d], (to, place.at[0]))
    def start(d, _):
        copy(d, tok).start()
        return 0
    lax.fori_loop(1, count, start, 0)
    got[place.core, tok // 2] = y_ref[0:8, pl.ds(pl.multiple_of((tok // 4) * 128, 128), 128)]
    def done(d, _):
        copy(d, lax.rem(tok + count - d, count)).wait_recv()
        return 0
    lax.fori_loop(1, count, done, 0)
    for k in range(2):
        flat[:, 128 * k:128 * (k + 1)] = got[k].reshape(128, 128).T * scale
    o_ref[...] = flat[pl.ds(pl.multiple_of(lax.rem(tok, 4) * 32, 32), 32)]
    def sent(d, _):
        copy(d, tok).wait_send()
        return 0
    lax.fori_loop(1, count, sent, 0)

def swap(y, scale):
    dma = pltpu.SemaphoreType.DMA
    return pl.pallas_call(
        functools.partial(swap_kernel, scale),
        out_shape=jax.ShapeDtypeStruct((32, 256), F32),
        in_specs=[pl.BlockSpec(memory_space=pltpu.VMEM)],
        out_specs=pl.BlockSpec(memory_space=pltpu.VMEM),
        scratch_shapes=[pltpu.VMEM((2, 16, 8, 128), F32), pltpu.VMEM((128, 256), F32), dma((32,)), dma((32,))],
        compiler_params=pltpu.CompilerParams(collective_id=2, has_side_effects=True),
        cost_estimate=pl.CostEstimate(flops=0, bytes_accessed=1 << 20, transcendentals=0),
    )(y)

BLK = 128

def split(x):
    hi = x.astype(BF16)
    return hi, (x - hi.astype(F32)).astype(BF16)

def mm_t(a, b):
    return lax.dot_general(a, b, (((1,), (1,)), ((), ())), preferred_element_type=F32)

def mm3_t(a, b):
    (ah, al), (bh, bl) = a, b
    return mm_t(ah, bh) + (mm_t(ah, bl) + mm_t(al, bh))

def inverse_factor(m):
    n = m.shape[0]
    nb = n // 8
    sub = lax.broadcasted_iota(jnp.int32, (8, n), 0)
    lane = lax.broadcasted_iota(jnp.int32, (8, n), 1)
    row = lambda v, i: jnp.broadcast_to(v[i:i + 1], (8, n))
    col = lambda v, i: jnp.broadcast_to(v[:, i:i + 1], (8, n))
    z = [m[8 * q:8 * q + 8] for q in range(nb)]
    diag = [col(z[0], k) for k in range(8)]
    out = []
    for s in range(nb):
        at = 8 * s
        inside = (lane >= at) & (lane < at + 8)
        zs = jnp.where(inside, jnp.where(lane == at + sub, 1.0, 0.0), z[s])
        more = s + 1 < nb
        if more:
            below = [col(z[s + 1], at + k) for k in range(8)]
            ahead = [col(z[s + 1], at + 8 + k) for k in range(8)]
        l = [[None] * 8 for _ in range(8)]
        r, x, c = [], [], []
        w = None
        for k in range(8):
            r.append(lax.rsqrt(row(diag[k], k)))
            dk = diag[k] * r[k]
            for j in range(k + 1, 8):
                l[j][k] = row(diag[k], j) * r[k]
                diag[j] = diag[j] - dk * l[j][k]
            if more:
                ck = below[k]
                for j in range(k):
                    ck = ck - c[j] * l[k][j]
                c.append(ck * r[k])
                for j in range(8):
                    ahead[j] = ahead[j] - c[k] * row(c[k], j)
            xk = row(zs, k)
            for j in range(k):
                xk = xk - l[k][j] * x[j]
            x.append(xk * r[k])
            w = x[k] if w is None else jnp.where(sub == k, x[k], w)
        out.append(jnp.where(lane < at + 8, w, 0.0))
        if more:
            diag = ahead
            zq = jnp.where(inside, 0.0, z[s + 1])
            for k in range(8):
                zq = zq - c[k] * x[k]
            z[s + 1] = zq
        if s + 2 < nb:
            y = [None] * 8
            for k in range(7, -1, -1):
                yk = x[k]
                for i in range(7, k, -1):
                    yk = yk - l[i][k] * y[i]
                y[k] = yk * r[k]
            for q in range(s + 2, nb):
                zq = jnp.where(inside, 0.0, z[q])
                for k in range(7, -1, -1):
                    zq = zq - col(z[q], at + k) * y[k]
                z[q] = zq
    return jnp.concatenate(out, 0)
def chol_body(n, extra, e_ref, lh, ll):
    total = n + extra
    nb = n // BLK
    for b in range(nb):
        r0, r1 = b * BLK, (b + 1) * BLK
        w = split(inverse_factor(e_ref[r0:r1, r0:r1]))
        for c in range(b + 1, nb + 1):
            lo, hi = c * BLK, min((c + 1) * BLK, total)
            x = mm3_t(split(e_ref[lo:hi, r0:r1]), w)
            if c == nb:
                e_ref[lo:hi, r0:r1] = x
            xh, xl = split(x)
            lh[lo:hi, :] = xh
            ll[lo:hi, :] = xl
        for c in range(b + 1, nb):
            lo = c * BLK
            e_ref[lo:total, lo:lo + BLK] -= mm3_t((lh[lo:total], ll[lo:total]), (lh[lo:lo + BLK], ll[lo:lo + BLK]))

def unpack(g_ref, e, sem):
    copies = []
    for i, (half, lane) in enumerate(G_PLACES):
        width = 128 * (i + 1)
        for core in range(2):
            src = g_ref.at[core, 256 * half:256 * (half + 1), lane:lane + width]
            copies.append(pltpu.make_async_copy(src, e.at[256 * i:256 * (i + 1), core * width:(core + 1) * width], sem.at[2 * i + core]))
    return copies

def kernel(n, extra, g_ref, c_ref, o_ref, e, lh, ll, sem):
    copies = [pltpu.make_async_copy(c_ref, e.at[n:n + extra], sem.at[8])] + unpack(g_ref, e, sem)
    for c in copies:
        c.start()
    for c in copies:
        c.wait()
    chol_body(n, extra, e, lh, ll)
    o_ref[...] = e[n:n + extra, :]

def solve(g, ct, **kw):
    extra, n = ct.shape
    return pl.pallas_call(
        functools.partial(kernel, n, extra),
        out_shape=jax.ShapeDtypeStruct((extra, n), F32),
        in_specs=[pl.BlockSpec(memory_space=pl.ANY)] * 2,
        out_specs=pl.BlockSpec(memory_space=pltpu.VMEM),
        scratch_shapes=[pltpu.VMEM((n + extra, n), F32), pltpu.VMEM((n + extra, BLK), BF16), pltpu.VMEM((n + extra, BLK), BF16), pltpu.SemaphoreType.DMA((9,))],
        compiler_params=pltpu.CompilerParams(vmem_limit_bytes=60 << 20),
        cost_estimate=pl.CostEstimate(flops=2_000_000_000, bytes_accessed=8 << 20, transcendentals=1024),
        **kw,
    )(g, ct)


def shards(samples, lengths, sketch):
    total, mine = front(lengths, samples, sketch)
    y = solve(total.reshape(2, 512, 640), mine)
    scale = math.sqrt(sketch.shape[1] / (samples.shape[0] // 2 * lax.axis_size("tok")))
    return swap(y, scale)


def solution(mesh):
    in_specs = (P("tok", "col"), P(), P())
    out_specs = P("tok", "col")
    return jax.shard_map(shards, mesh=mesh, in_specs=in_specs, out_specs=out_specs, check_vma=False)
```

profile of v0, /device:TPU:1, one launch (start us, length us, event | category | flops | bytes accessed | tf_op | source)
XLA Modules:
  0.0 116.4 jit_solution(9028475405171222983)
XLA Ops:
  0.0 1.4 %copy.4.len_ref = s32[32,16]{1,0:T(8,128)} copy(s32[32,16]{0,1:T(8,128)} %param.4) | data formatting | bytes 4096 | tf_op args[1]
  1.4 76.0 %shard_map.37 = (f32[2,4,4,4,8,640]{5,4,3,2,1,0:T(8,128)}, f32[16,1024]{1,0:T(8,128)}) custom-call(s32[32,16]{1,0:T(8,128)} %copy.4.len_ref, bf16[4,1024,256]{2,1,0:T(8,128)(2,1)} %bitcast.2, bf16[1024,1024]{1,0:T(8,128)(2,1)} %sk_ref.1), custom_call_target="tpu_custom_call" | custom-call | flops 12999999488 | bytes 8388608 | tf_op jit(solution)/shard_map/pallas_call | solution.py:354
  77.4 27.3 %shard_map.38.y_ref = f32[16,1024]{1,0:T(8,128)} custom-call(f32[2,512,640]{2,1,0:T(8,128)} %bitcast.3, f32[16,1024]{1,0:T(8,128)} %get-tuple-element.8.c_ref), custom_call_target="tpu_custom_call" | custom-call | flops 2000000000 | bytes 8388608 | tf_op jit(solution)/shard_map/pallas_call | solution.py:521
  104.6 10.4 %shard_map.39 = f32[32,256]{1,0:T(8,128)} custom-call(f32[16,1024]{1,0:T(8,128)} %shard_map.38.y_ref), custom_call_target="tpu_custom_call" | custom-call | bytes 1048576 | tf_op jit(solution)/shard_map/pallas_call | solution.py:401
  115.0 1.4 %copy.6 = f32[32,256]{1,0:T(8,128)} copy(f32[32,256]{1,0:T(8,128)} %shard_map.39) | data formatting | bytes 65536
where the time goes:
time: 117 us; the launch traced here: 116 us
  Pallas kernels  114 us (97%)
  local copies, waits for them, and re-layouts  2.75 us (2%)
    pallas_call x1, Pallas kernels, front(): pl.pallas_call(front_kernel, out_shape=(jax.ShapeDtypeStruct((2, 4, 4, 4,...  76 us
    pallas_call x1, Pallas kernels, solve(): pl.pallas_call(functools.partial(kernel, n, extra), out_shape=jax.ShapeDt...  27.3 us
    pallas_call x1, Pallas kernels, swap(): pl.pallas_call(functools.partial(swap_kernel, scale), out_shape=jax.Shape...  10.4 us
    unnamed x2, local copies, waits for them, and re-layouts  2.75 us

commit v1 on v0

--- a/solution.py
+++ b/solution.py
@@ -14,6 +14,8 @@
 C_STREAMS = ((0, 256), (256, 384), (640, 384))
 G_PLACES = ((0, 512), (1, 384), (1, 0), (0, 0))
 SUBS = 4
+TOKS = 32
+BLK = 128
 
 class Place:
     def __init__(self):
@@ -46,11 +48,13 @@
 
 def greet(place):
     barrier = pltpu.get_barrier_semaphore()
-    pl.semaphore_signal(barrier, inc=1, device_id=place.mate(), device_id_type=MESH)
-    for axis in range(3):
-        for d in range(1, 4):
-            pl.semaphore_signal(barrier, inc=1, device_id=place.peer(axis, d), device_id_type=MESH)
-    pl.semaphore_wait(barrier, 10)
+    def hello(d, _):
+        pl.semaphore_signal(barrier, inc=1, device_id=(lax.rem(place.tok + d, TOKS), place.at[0]), device_id_type=MESH)
+        return 0
+    lax.fori_loop(1, TOKS, hello, 0)
+    for d in range(1, 4):
+        pl.semaphore_signal(barrier, inc=1, device_id=place.peer(0, d), device_id_type=MESH)
+    pl.semaphore_wait(barrier, TOKS + 2)
 
 class Reduction:
     def __init__(self, place, streams, acc, r1, a1, r2, a2, r3, a3, ps, pr):
@@ -106,11 +110,10 @@
             c.wait_send()
 
 class Spread:
-    def __init__(self, red, full, out, ss, rs, fs, fr, ws):
+    def __init__(self, red, full, ss, rs, fs, fr):
         self.red, self.full, self.place = red, full, red.place
-        self.ss, self.rs, self.fs, self.fr, self.ws = ss, rs, fs, fr, ws
-        self.out = out
-        self.sends, self.writes = [], []
+        self.ss, self.rs, self.fs, self.fr = ss, rs, fs, fr
+        self.sends = []
 
     def region(self, s, fixed, core):
         idx = [slice(None)] * 3
@@ -154,31 +157,19 @@
         reg = self.region(s, f, core)
         return remote(reg, reg, self.fs.at[s, d], self.fr.at[s, d], self.place.mate())
 
-    def write(self, s, d, core):
-        f, _ = self.fixed(s, 2, d)
-        idx = [slice(None)] * 3
-        for axis, p in f.items():
-            idx[axis] = p
-        idx = (core,) + tuple(idx) + (slice(None), pl.ds(*self.red.streams[s]))
-        c = pltpu.make_async_copy(self.full.at[idx], self.out.at[idx], self.ws.at[s, d, 0 if core is self.place.core else 1])
-        c.start()
-        self.writes.append(c)
-
     def forward(self, s, d):
         c = self.passing(s, d, self.place.core)
         c.start()
         self.sends.append(c)
-        self.write(s, d, self.place.core)
 
     def finish(self):
         for d in (0, 1, 3, 2):
             for s in range(3):
                 self.passing(s, d, 1 - self.place.core).wait_recv()
-                self.write(s, d, 1 - self.place.core)
+
+    def sent(self):
         for c in self.sends:
             c.wait_send()
-        for c in self.writes:
-            c.wait()
 
 class Rows:
     def __init__(self, place, x, held, loc, zs, zr, ms, mr):
@@ -241,7 +232,7 @@
         for a in range(8):
             wcol[k, 128 * a:128 * (a + 1)] = jnp.broadcast_to(wt[:, a:a + 1], (128, 128))
 
-def front_kernel(len_ref, x_ref, sk_ref, go_ref, co_ref, held, omega, wcol, sh, sl, gs, cs, full, ss, rs, fs, fr, ws, loc, zs, zr, ms, mr, osem):
+def whole_kernel(scale, len_ref, x_ref, sk_ref, o_ref, held, omega, wcol, sh, sl, gs, cs, full, ext, lh, ll, wh, wl, got, flat, ss, rs, fs, fr, loc, zs, zr, ms, mr, osem, ys, yr):
     place = Place()
     core = place.core
     rows = Rows(place, x_ref, held, loc, zs, zr, ms, mr)
@@ -302,12 +293,10 @@
         return 0
 
     lax.fori_loop(0, SUBS, cross, 0)
-    sp = Spread(g, full, go_ref, ss, rs, fs, fr, ws)
+    sp = Spread(g, full, ss, rs, fs, fr)
     for s in range(3):
         g.gather(0, s)
         g.send(1, s)
-    for s in range(3):
-        c.send(0, s)
     for s in range(3):
         g.gather(1, s)
         g.share(s)
@@ -315,25 +304,42 @@
         sp.seed(s)
         sp.send(1, s)
     for s in range(3):
-        c.gather(0, s)
-        c.send(1, s)
-    for s in range(3):
         sp.wait(1, s)
         sp.send(2, s)
         sp.forward(s, 0)
     for s in range(3):
-        c.gather(1, s)
-        c.send(2, s)
+        c.send(0, s)
     for d in (1, 3, 2):
         for s in range(3):
             sp.arrived(2, s, d)
             sp.forward(s, d)
-    for s in range(3):
-        c.gather(2, s)
-        o, n = C_STREAMS[s]
-        co_ref[0:8, o:o + n] = c.a[2][s][...]
-    co_ref[8:16, :] = jnp.zeros((8, omega.shape[1]), F32)
     sp.finish()
+    sp.sent()
+
+    result = Result(place, ext, got, flat, ys, yr)
+
+    def meanwhile(b):
+        if b == 2:
+            for s in range(3):
+                c.gather(0, s)
+                c.send(1, s)
+        if b == 3:
+            for s in range(3):
+                c.gather(1, s)
+                c.send(2, s)
+        if b == 5:
+            for s in range(3):
+                c.gather(2, s)
+                o, n = C_STREAMS[s]
+                ext[0:8, o:o + n] = c.a[2][s][...]
+            ext[8:16, :] = jnp.zeros((8, omega.shape[1]), F32)
+        if b >= 5:
+            for k in range(0 if b == 5 else b, b + 1):
+                extend(k, ext, lh, ll, wh, wl)
+                result.send(k)
+
+    factor(full, lh, ll, wh, wl, meanwhile)
+    result.finish(o_ref, scale)
     rows.finish()
     g.finish()
     c.finish()
@@ -346,69 +352,37 @@
     return [pltpu.VMEM((4, 4, 4, 8, lanes), F32), per((3, 4, 4)), per((4, 4)), per((3, 4)), per((4,)), per((3,) + last), per(last),
             dma((3, 3, 3)), dma((3, 3, 3))]
 
-def front(lengths, samples, sketch):
-    dma = pltpu.SemaphoreType.DMA
-    rows, feats = samples.shape
-    width = sketch.shape[1]
-    chunk = rows // 4
-    return pl.pallas_call(
-        front_kernel,
-        out_shape=(jax.ShapeDtypeStruct((2, 4, 4, 4, 8, 640), F32), jax.ShapeDtypeStruct((16, width), F32)),
-        in_specs=[pl.BlockSpec(memory_space=pltpu.SMEM), pl.BlockSpec(memory_space=pl.ANY), pl.BlockSpec(memory_space=pl.ANY)],
-        out_specs=(pl.BlockSpec(memory_space=pl.ANY), pl.BlockSpec(memory_space=pltpu.VMEM)),
-        scratch_shapes=[pltpu.VMEM((2, 4, chunk, feats), BF16), pltpu.VMEM(sketch.shape, BF16), pltpu.VMEM((2, chunk, 128), F32),
-                        pltpu.VMEM((2 * chunk, width), BF16), pltpu.VMEM((2 * chunk, width), BF16),
-                        reduce_scratch(G_STREAMS, (4,)), reduce_scratch(C_STREAMS, ()), pltpu.VMEM((2, 4, 4, 4, 8, 640), F32),
-                        dma((3, 3, 3)), dma((3, 3, 3)), dma((3, 4)), dma((3, 4)), dma((3, 4, 2)),
-                        dma((SUBS,)), dma((SUBS, 3)), dma((SUBS, 3)), dma((SUBS, 4)), dma((SUBS, 4)), dma((1,))],
-        compiler_params=pltpu.CompilerParams(collective_id=1, has_side_effects=True, vmem_limit_bytes=56 << 20),
-        cost_estimate=pl.CostEstimate(flops=13_000_000_000, bytes_accessed=8 << 20, transcendentals=0),
-    )(lengths, samples.reshape(4, chunk, feats), sketch)
-
-def swap_kernel(scale, y_ref, o_ref, got, flat, ssem, rsem):
-    place = Place()
-    tok = place.tok
-    barrier = pltpu.get_barrier_semaphore()
-    count = 32
-    def hello(d, _):
-        pl.semaphore_signal(barrier, inc=1, device_id=(lax.rem(tok + d, count), place.at[0]), device_id_type=MESH)
-        return 0
-    lax.fori_loop(1, count, hello, 0)
-    pl.semaphore_wait(barrier, count - 1)
-    def copy(d, owner):
-        to = lax.rem(tok + d, count)
-        lanes = pl.ds(pl.multiple_of((to // 4) * 128, 128), 128)
-        return remote(y_ref.at[0:8, lanes], got.at[lax.rem(owner, 2), owner // 2], ssem.at[d], rsem.at[d], (to, place.at[0]))
-    def start(d, _):
-        copy(d, tok).start()
-        return 0
-    lax.fori_loop(1, count, start, 0)
-    got[place.core, tok // 2] = y_ref[0:8, pl.ds(pl.multiple_of((tok // 4) * 128, 128), 128)]
-    def done(d, _):
-        copy(d, lax.rem(tok + count - d, count)).wait_recv()
-        return 0
-    lax.fori_loop(1, count, done, 0)
-    for k in range(2):
-        flat[:, 128 * k:128 * (k + 1)] = got[k].reshape(128, 128).T * scale
-    o_ref[...] = flat[pl.ds(pl.multiple_of(lax.rem(tok, 4) * 32, 32), 32)]
-    def sent(d, _):
-        copy(d, tok).wait_send()
-        return 0
-    lax.fori_loop(1, count, sent, 0)
-
-def swap(y, scale):
-    dma = pltpu.SemaphoreType.DMA
-    return pl.pallas_call(
-        functools.partial(swap_kernel, scale),
-        out_shape=jax.ShapeDtypeStruct((32, 256), F32),
-        in_specs=[pl.BlockSpec(memory_space=pltpu.VMEM)],
-        out_specs=pl.BlockSpec(memory_space=pltpu.VMEM),
-        scratch_shapes=[pltpu.VMEM((2, 16, 8, 128), F32), pltpu.VMEM((128, 256), F32), dma((32,)), dma((32,))],
-        compiler_params=pltpu.CompilerParams(collective_id=2, has_side_effects=True),
-        cost_estimate=pl.CostEstimate(flops=0, bytes_accessed=1 << 20, transcendentals=0),
-    )(y)
-
-BLK = 128
+class Result:
+    def __init__(self, place, ext, got, flat, ys, yr):
+        self.place, self.ext, self.got, self.flat, self.ys, self.yr = place, ext, got, flat, ys, yr
+
+    def copy(self, to, owner, b):
+        return remote(self.ext.at[0:8, BLK * b:BLK * (b + 1)], self.got.at[lax.rem(owner, 2), owner // 2], self.ys.at[to], self.yr.at[owner], (to, self.place.at[0]))
+
+    def send(self, b):
+        tok = self.place.tok
+        for to in range(4 * b, 4 * b + 4):
+            @pl.when(tok != to)
+            def _():
+                self.copy(to, tok, b).start()
+        @pl.when(tok // 4 == b)
+        def _():
+            self.got[self.place.core, tok // 2] = self.ext[0:8, BLK * b:BLK * (b + 1)]
+
+    def finish(self, o_ref, scale):
+        tok = self.place.tok
+        def landed(d, _):
+            src = lax.rem(tok + d, TOKS)
+            self.copy(src, src, 0).wait_recv()
+            return 0
+        lax.fori_loop(1, TOKS, landed, 0)
+        for k in range(2):
+            self.flat[:, 128 * k:128 * (k + 1)] = self.got[k].reshape(128, 128).T * scale
+        o_ref[...] = self.flat[pl.ds(pl.multiple_of(lax.rem(tok, 4) * 32, 32), 32)]
+        def sent(d, _):
+            self.copy(lax.rem(tok + d, TOKS), tok, 0).wait_send()
+            return 0
+        lax.fori_loop(1, TOKS, sent, 0)
 
 def split(x):
     hi = x.astype(BF16)
@@ -480,61 +454,66 @@
                     zq = zq - col(z[q], at + k) * y[k]
                 z[q] = zq
     return jnp.concatenate(out, 0)
-def chol_body(n, extra, e_ref, lh, ll):
-    total = n + extra
-    nb = n // BLK
+def block(r, c):
+    i = r // 2
+    width = 128 * (i + 1)
+    core = (128 * c) // width
+    half, lane = G_PLACES[i]
+    lane += 128 * c - core * width
+    return (core, 2 * half + r % 2, slice(None), slice(None), slice(None), slice(lane, lane + BLK))
+
+def factor(full, lh, ll, wh, wl, meanwhile):
+    nb = wh.shape[0]
+    get = lambda r, c: full[block(r, c)].reshape(BLK, BLK)
     for b in range(nb):
-        r0, r1 = b * BLK, (b + 1) * BLK
-        w = split(inverse_factor(e_ref[r0:r1, r0:r1]))
-        for c in range(b + 1, nb + 1):
-            lo, hi = c * BLK, min((c + 1) * BLK, total)
-            x = mm3_t(split(e_ref[lo:hi, r0:r1]), w)
-            if c == nb:
-                e_ref[lo:hi, r0:r1] = x
-            xh, xl = split(x)
-            lh[lo:hi, :] = xh
-            ll[lo:hi, :] = xl
+        w = split(inverse_factor(get(b, b)))
+        wh[b], wl[b] = w
+        for r in range(b + 1, nb):
+            at = slice(r * BLK, (r + 1) * BLK)
+            lh[b, at], ll[b, at] = split(mm3_t(split(get(r, b)), w))
         for c in range(b + 1, nb):
-            lo = c * BLK
-            e_ref[lo:total, lo:lo + BLK] -= mm3_t((lh[lo:total], ll[lo:total]), (lh[lo:lo + BLK], ll[lo:lo + BLK]))
-
-def unpack(g_ref, e, sem):
-    copies = []
-    for i, (half, lane) in enumerate(G_PLACES):
-        width = 128 * (i + 1)
-        for core in range(2):
-            src = g_ref.at[core, 256 * half:256 * (half + 1), lane:lane + width]
-            copies.append(pltpu.make_async_copy(src, e.at[256 * i:256 * (i + 1), core * width:(core + 1) * width], sem.at[2 * i + core]))
-    return copies
-
-def kernel(n, extra, g_ref, c_ref, o_ref, e, lh, ll, sem):
-    copies = [pltpu.make_async_copy(c_ref, e.at[n:n + extra], sem.at[8])] + unpack(g_ref, e, sem)
-    for c in copies:
-        c.start()
-    for c in copies:
-        c.wait()
-    chol_body(n, extra, e, lh, ll)
-    o_ref[...] = e[n:n + extra, :]
-
-def solve(g, ct, **kw):
-    extra, n = ct.shape
+            below, at = slice(c * BLK, nb * BLK), slice(c * BLK, (c + 1) * BLK)
+            v = mm3_t((lh[b, below], ll[b, below]), (lh[b, at], ll[b, at]))
+            for r in range(c, nb):
+                idx = block(r, c)
+                full[idx] = full[idx] - v[(r - c) * BLK:(r - c + 1) * BLK].reshape(4, 4, 8, BLK)
+        meanwhile(b)
+
+def extend(b, ext, lh, ll, wh, wl):
+    at, rest = slice(b * BLK, (b + 1) * BLK), slice((b + 1) * BLK, ext.shape[1])
+    y = mm3_t(split(ext[:, at]), (wh[b], wl[b]))
+    ext[:, at] = y
+    if rest.start < rest.stop:
+        ext[:, rest] = ext[:, rest] - mm3_t(split(y), (lh[b, rest], ll[b, rest]))
+
+def whole(lengths, samples, sketch, scale):
+    dma = pltpu.SemaphoreType.DMA
+    rows, feats = samples.shape
+    width = sketch.shape[1]
+    chunk = rows // 4
+    nb = width // BLK
     return pl.pallas_call(
-        functools.partial(kernel, n, extra),
-        out_shape=jax.ShapeDtypeStruct((extra, n), F32),
-        in_specs=[pl.BlockSpec(memory_space=pl.ANY)] * 2,
+        functools.partial(whole_kernel, scale),
+        out_shape=jax.ShapeDtypeStruct((width // TOKS, feats), F32),
+        in_specs=[pl.BlockSpec(memory_space=pltpu.SMEM), pl.BlockSpec(memory_space=pl.ANY), pl.BlockSpec(memory_space=pl.ANY)],
         out_specs=pl.BlockSpec(memory_space=pltpu.VMEM),
-        scratch_shapes=[pltpu.VMEM((n + extra, n), F32), pltpu.VMEM((n + extra, BLK), BF16), pltpu.VMEM((n + extra, BLK), BF16), pltpu.SemaphoreType.DMA((9,))],
-        compiler_params=pltpu.CompilerParams(vmem_limit_bytes=60 << 20),
-        cost_estimate=pl.CostEstimate(flops=2_000_000_000, bytes_accessed=8 << 20, transcendentals=1024),
-        **kw,
-    )(g, ct)
+        scratch_shapes=[pltpu.VMEM((2, 4, chunk, feats), BF16), pltpu.VMEM(sketch.shape, BF16), pltpu.VMEM((2, chunk, 128), F32),
+                        pltpu.VMEM((2 * chunk, width), BF16), pltpu.VMEM((2 * chunk, width), BF16),
+                        reduce_scratch(G_STREAMS, (4,)), reduce_scratch(C_STREAMS, ()), pltpu.VMEM((2, 4, 4, 4, 8, 640), F32),
+                        pltpu.VMEM((16, width), F32), pltpu.VMEM((nb, width, BLK), BF16), pltpu.VMEM((nb, width, BLK), BF16),
+                        pltpu.VMEM((nb, BLK, BLK), BF16), pltpu.VMEM((nb, BLK, BLK), BF16),
+                        pltpu.VMEM((2, 16, 8, BLK), F32), pltpu.VMEM((BLK, feats), F32),
+                        dma((3, 3, 3)), dma((3, 3, 3)), dma((3, 4)), dma((3, 4)),
+                        dma((SUBS,)), dma((SUBS, 3)), dma((SUBS, 3)), dma((SUBS, 4)), dma((SUBS, 4)), dma((1,)),
+                        dma((TOKS,)), dma((TOKS,))],
+        compiler_params=pltpu.CompilerParams(collective_id=1, has_side_effects=True, vmem_limit_bytes=60 << 20),
+        cost_estimate=pl.CostEstimate(flops=15_000_000_000, bytes_accessed=8 << 20, transcendentals=0),
+    )(lengths, samples.reshape(4, chunk, feats), sketch)
 
 
 def shards(samples, lengths, sketch):
-    total, mine = front(lengths, samples, sketch)
-    y = solve(total.reshape(2, 512, 640), mine)
     scale = math.sqrt(sketch.shape[1] / (samples.shape[0] // 2 * lax.axis_size("tok")))
-    return swap(y, scale)
+    return whole(lengths, samples, sketch, scale)
 
 
 def solution(mesh):

time: 117 us -> 112 us (0.957)
  Pallas kernels: 114 us -> 108 us
    pallas_call x3 -> x1, Pallas kernels: 114 us -> 108 us  [whole(): pl.pallas_call(functools.partial(whole_kernel, scale), out_shape=jax.Shap...]
where the time goes in v1:
time: 112 us; the launch traced here: 110 us
  Pallas kernels  108 us (96%)
  local copies, waits for them, and re-layouts  2.75 us (2%)
    pallas_call x1, Pallas kernels, whole(): pl.pallas_call(functools.partial(whole_kernel, scale), out_shape=jax.Shap...  108 us
    unnamed x2, local copies, waits for them, and re-layouts  2.75 us

profile of v1, /device:TPU:1, one launch (start us, length us, event | category | flops | bytes accessed | tf_op | source)
XLA Modules:
  0.0 110.5 jit_solution(898715787208009933)
XLA Ops:
  0.0 1.4 %copy.4.len_ref = s32[32,16]{1,0:T(8,128)} copy(s32[32,16]{0,1:T(8,128)} %param.4) | data formatting | bytes 4096 | tf_op args[1]
  1.4 107.7 %shard_map.37 = f32[32,256]{1,0:T(8,128)} custom-call(s32[32,16]{1,0:T(8,128)} %copy.4.len_ref, bf16[4,1024,256]{2,1,0:T(8,128)(2,1)} %bitcast.1, bf16[1024,1024]{1,0:T(8,128)(2,1)} %sk_ref.1), custom_call_target="tpu_custom_call" | custom-call | flops 15000000512 | bytes 8388608 | tf_op jit(solution)/shard_map/pallas_call | solution.py:495
  109.1 1.4 %copy.6 = f32[32,256]{1,0:T(8,128)} copy(f32[32,256]{1,0:T(8,128)} %shard_map.37) | data formatting | bytes 65536

commit v2 on v1

--- a/solution.py
+++ b/solution.py
@@ -13,7 +13,7 @@
 G_STREAMS = ((0, 256), (256, 256), (512, 128))
 C_STREAMS = ((0, 256), (256, 384), (640, 384))
 G_PLACES = ((0, 512), (1, 384), (1, 0), (0, 0))
-SUBS = 4
+SUBS = 8
 TOKS = 32
 BLK = 128
 
@@ -162,10 +162,9 @@
         c.start()
         self.sends.append(c)
 
-    def finish(self):
+    def finish(self, s):
         for d in (0, 1, 3, 2):
-            for s in range(3):
-                self.passing(s, d, 1 - self.place.core).wait_recv()
+            self.passing(s, d, 1 - self.place.core).wait_recv()
 
     def sent(self):
         for c in self.sends:
@@ -220,11 +219,11 @@
     assert rows == 1024
     pos = place.at[0] * rows + lax.broadcasted_iota(jnp.int32, (8, 128), 0) * 128 + lax.broadcasted_iota(jnp.int32, (8, 128), 1)
     for k in range(2):
-        buf = place.tok - place.core + k
+        own = lengths[pl.ds(place.tok - place.core + k, 1), :]
         start = jnp.zeros((8, 128), jnp.int32)
         w = jnp.zeros((8, 128), F32)
         for s in range(lengths.shape[1]):
-            count = jnp.full((8, 128), lengths[buf, s], jnp.int32)
+            count = jnp.broadcast_to(own[:, s:s + 1], (8, 128))
             per = lax.rsqrt(1.0 + 4.0 * count.astype(F32) / float(2 * rows))
             w = w + jnp.where((pos >= start) & (pos < start + count), per, 0.0)
             start = start + count
@@ -284,12 +283,11 @@
 
     def cross(sub, _):
         mine = pl.ds(pl.multiple_of(core * 128, 128), 128)
-        for k in range(2):
-            which = core if k == 0 else 1 - core
-            x = jnp.concatenate([held[which, z, pl.ds(sub * step, step), mine] for z in range(4)], 1)
-            at = pl.ds((2 * sub + k) * step, step)
-            v = over_rows(x, sh[at]) + over_rows(x, sl[at])
-            c.acc[...] += v.reshape(4, 4, 4, 8, omega.shape[1])
+        x = jnp.concatenate([
+            jnp.concatenate([held[which, z, pl.ds(sub * step, step), mine] for z in range(4)], 1) for which in (core, 1 - core)], 0)
+        at = pl.ds(2 * sub * step, 2 * step)
+        v = over_rows(x, sh[at]) + over_rows(x, sl[at])
+        c.acc[...] += v.reshape(4, 4, 4, 8, omega.shape[1])
         return 0
 
     lax.fori_loop(0, SUBS, cross, 0)
@@ -297,6 +295,8 @@
     for s in range(3):
         g.gather(0, s)
         g.send(1, s)
+    for s in range(3):
+        c.send(0, s)
     for s in range(3):
         g.gather(1, s)
         g.share(s)
@@ -308,37 +308,38 @@
         sp.send(2, s)
         sp.forward(s, 0)
     for s in range(3):
-        c.send(0, s)
+        c.gather(0, s)
+        c.send(1, s)
     for d in (1, 3, 2):
-        for s in range(3):
+        for s in (2, 0, 1):
             sp.arrived(2, s, d)
             sp.forward(s, d)
-    sp.finish()
-    sp.sent()
+    sp.finish(2)
+
+    def settled():
+        sp.finish(0)
+        sp.finish(1)
+        sp.sent()
 
     result = Result(place, ext, got, flat, ys, yr)
 
     def meanwhile(b):
-        if b == 2:
-            for s in range(3):
-                c.gather(0, s)
-                c.send(1, s)
-        if b == 3:
+        if b == 1:
             for s in range(3):
                 c.gather(1, s)
                 c.send(2, s)
-        if b == 5:
+        if b == 3:
             for s in range(3):
                 c.gather(2, s)
                 o, n = C_STREAMS[s]
                 ext[0:8, o:o + n] = c.a[2][s][...]
             ext[8:16, :] = jnp.zeros((8, omega.shape[1]), F32)
-        if b >= 5:
-            for k in range(0 if b == 5 else b, b + 1):
+        if b >= 3:
+            for k in range(0 if b == 3 else b, b + 1):
                 extend(k, ext, lh, ll, wh, wl)
                 result.send(k)
 
-    factor(full, lh, ll, wh, wl, meanwhile)
+    factor(full, lh, ll, wh, wl, settled, meanwhile)
     result.finish(o_ref, scale)
     rows.finish()
     g.finish()
@@ -462,12 +463,14 @@
     lane += 128 * c - core * width
     return (core, 2 * half + r % 2, slice(None), slice(None), slice(None), slice(lane, lane + BLK))
 
-def factor(full, lh, ll, wh, wl, meanwhile):
+def factor(full, lh, ll, wh, wl, settled, meanwhile):
     nb = wh.shape[0]
     get = lambda r, c: full[block(r, c)].reshape(BLK, BLK)
     for b in range(nb):
         w = split(inverse_factor(get(b, b)))
         wh[b], wl[b] = w
+        if b == 0:
+            settled()
         for r in range(b + 1, nb):
             at = slice(r * BLK, (r + 1) * BLK)
             lh[b, at], ll[b, at] = split(mm3_t(split(get(r, b)), w))
@@ -495,7 +498,7 @@
     return pl.pallas_call(
         functools.partial(whole_kernel, scale),
         out_shape=jax.ShapeDtypeStruct((width // TOKS, feats), F32),
-        in_specs=[pl.BlockSpec(memory_space=pltpu.SMEM), pl.BlockSpec(memory_space=pl.ANY), pl.BlockSpec(memory_space=pl.ANY)],
+        in_specs=[pl.BlockSpec(memory_space=pltpu.VMEM), pl.BlockSpec(memory_space=pl.ANY), pl.BlockSpec(memory_space=pl.ANY)],
         out_specs=pl.BlockSpec(memory_space=pltpu.VMEM),
         scratch_shapes=[pltpu.VMEM((2, 4, chunk, feats), BF16), pltpu.VMEM(sketch.shape, BF16), pltpu.VMEM((2, chunk, 128), F32),
                         pltpu.VMEM((2 * chunk, width), BF16), pltpu.VMEM((2 * chunk, width), BF16),

time: 112 us -> 115 us (1.027)
  Pallas kernels: 108 us -> 111 us
    pallas_call x1, Pallas kernels: 108 us -> 111 us  [whole(): pl.pallas_call(functools.partial(whole_kernel, scale), out_shape=jax.Shap...]
where the time goes in v2:
time: 115 us; the launch traced here: 114 us
  Pallas kernels  111 us (97%)
  local copies, waits for them, and re-layouts  2.75 us (2%)
    pallas_call x1, Pallas kernels, whole(): pl.pallas_call(functools.partial(whole_kernel, scale), out_shape=jax.Shap...  111 us
    unnamed x2, local copies, waits for them, and re-layouts  2.75 us

profile of v2, /device:TPU:1, one launch (start us, length us, event | category | flops | bytes accessed | tf_op | source)
XLA Modules:
  0.0 114.1 jit_solution(10601302400568314502)
XLA Ops:
  0.0 1.4 %copy.4.len_ref = s32[32,16]{1,0:T(8,128)} copy(s32[32,16]{0,1:T(8,128)} %param.4) | data formatting | bytes 4096 | tf_op args[1]
  1.4 111.3 %shard_map.37 = f32[32,256]{1,0:T(8,128)} custom-call(s32[32,16]{1,0:T(8,128)} %copy.4.len_ref, bf16[4,1024,256]{2,1,0:T(8,128)(2,1)} %bitcast.1, bf16[1024,1024]{1,0:T(8,128)(2,1)} %sk_ref.1), custom_call_target="tpu_custom_call" | custom-call | flops 15000000512 | bytes 8388608 | tf_op jit(solution)/shard_map/pallas_call | solution.py:498
  112.7 1.4 %copy.6 = f32[32,256]{1,0:T(8,128)} copy(f32[32,256]{1,0:T(8,128)} %shard_map.37) | data formatting | bytes 65536

commit v3 on v2

--- a/solution.py
+++ b/solution.py
@@ -13,7 +13,7 @@
 G_STREAMS = ((0, 256), (256, 256), (512, 128))
 C_STREAMS = ((0, 256), (256, 384), (640, 384))
 G_PLACES = ((0, 512), (1, 384), (1, 0), (0, 0))
-SUBS = 8
+SUBS = 4
 TOKS = 32
 BLK = 128
 
@@ -296,8 +296,6 @@
         g.gather(0, s)
         g.send(1, s)
     for s in range(3):
-        c.send(0, s)
-    for s in range(3):
         g.gather(1, s)
         g.share(s)
     for s in range(3):
@@ -307,13 +305,12 @@
         sp.wait(1, s)
         sp.send(2, s)
         sp.forward(s, 0)
-    for s in range(3):
-        c.gather(0, s)
-        c.send(1, s)
     for d in (1, 3, 2):
         for s in (2, 0, 1):
             sp.arrived(2, s, d)
             sp.forward(s, d)
+    for s in range(3):
+        c.send(0, s)
     sp.finish(2)
 
     def settled():
@@ -324,18 +321,22 @@
     result = Result(place, ext, got, flat, ys, yr)
 
     def meanwhile(b):
-        if b == 1:
+        if b == 3:
+            for s in range(3):
+                c.gather(0, s)
+                c.send(1, s)
+        if b == 4:
             for s in range(3):
                 c.gather(1, s)
                 c.send(2, s)
-        if b == 3:
+        if b == 6:
             for s in range(3):
                 c.gather(2, s)
                 o, n = C_STREAMS[s]
                 ext[0:8, o:o + n] = c.a[2][s][...]
             ext[8:16, :] = jnp.zeros((8, omega.shape[1]), F32)
-        if b >= 3:
-            for k in range(0 if b == 3 else b, b + 1):
+        if b >= 6:
+            for k in range(0 if b == 6 else b, b + 1):
                 extend(k, ext, lh, ll, wh, wl)
                 result.send(k)
 

time: 115 us -> 106 us (0.922)
  Pallas kernels: 111 us -> 102 us
    pallas_call x1, Pallas kernels: 111 us -> 102 us  [whole(): pl.pallas_call(functools.partial(whole_kernel, scale), out_shape=jax.Shap...]
where the time goes in v3:
time: 106 us; the launch traced here: 105 us
  Pallas kernels  102 us (96%)
  local copies, waits for them, and re-layouts  2.75 us (3%)
    pallas_call x1, Pallas kernels, whole(): pl.pallas_call(functools.partial(whole_kernel, scale), out_shape=jax.Shap...  102 us
    unnamed x2, local copies, waits for them, and re-layouts  2.75 us

profile of v3, /device:TPU:1, one launch (start us, length us, event | category | flops | bytes accessed | tf_op | source)
XLA Modules:
  0.0 105.1 jit_solution(14122622858552380599)
XLA Ops:
  0.0 1.4 %copy.4.len_ref = s32[32,16]{1,0:T(8,128)} copy(s32[32,16]{0,1:T(8,128)} %param.4) | data formatting | bytes 4096 | tf_op args[1]
  1.4 102.4 %shard_map.37 = f32[32,256]{1,0:T(8,128)} custom-call(s32[32,16]{1,0:T(8,128)} %copy.4.len_ref, bf16[4,1024,256]{2,1,0:T(8,128)(2,1)} %bitcast.1, bf16[1024,1024]{1,0:T(8,128)(2,1)} %sk_ref.1), custom_call_target="tpu_custom_call" | custom-call | flops 15000000512 | bytes 8388608 | tf_op jit(solution)/shard_map/pallas_call | solution.py:499
  103.7 1.4 %copy.6 = f32[32,256]{1,0:T(8,128)} copy(f32[32,256]{1,0:T(8,128)} %shard_map.37) | data formatting | bytes 65536
